TPU v7x, 32 devices: a whole 2x2x4 slice. The times are simulated.
32 devices in a mesh: ctx: 8 (over y, x, core), dp: 4 (over z).
Axes of the slice: x: 2, y: 2, z: 4, core: 2. Of those that a mesh axis runs over, the one named last changes fastest.
Arguments:
- query: bfloat16 [4, 1536, 4096], P('dp', 'ctx'), may hold values from -6 to 6
- key_value: bfloat16 [4, 1536, 1024], P('dp', 'ctx'), may hold values from -6 to 6
- upstream: bfloat16 [4, 1536, 4096], P('dp', 'ctx'), may hold values from -6 to 6
- log_ratio: float32 [4, 1536], P('dp', 'ctx'), may hold values from -4 to 1
- doc_starts: int32 [4, 16], P('dp'), may hold values from 0 to 1536, as said below
- answer_counts: int32 [4, 16], P('dp'), may hold values from 0 to 768, as said below
Outputs:
- d_query: bfloat16 [4, 1536, 4096], P('dp', 'ctx')
- d_key_value: bfloat16 [4, 1536, 1024], P('dp', 'ctx')
Inputs may be any that keep to these rules, and one draw needn't show every extreme that they name: `doc_starts`: used slots come first; each sequence's documents start at the listed positions in rising order, the first at 0, together covering all 1536 positions; unused slots hold 1536; every document has 96 to 768 positions, and every sequence has a document of exactly 768 positions. A document's answer positions are its last answer_counts positions; a used slot holds half of the document's length (rounded down) up to all of it, an unused slot 0; every sequence has a document of 768 positions that are all answer positions.
All inputs are finite; a program needn't handle non-finite values.
Results may differ from a plain program's by a relative error of at most 0.011.
Values may be sent and summed in bfloat16 or wider, within the bound.
A program may use at most 64 MiB of HBM per device.

v0:
```python
from functools import partial

import jax
import jax.numpy as jnp
from jax import lax
from jax.sharding import PartitionSpec as P

HQ = 32
HK = 4
DH = 128
SPAN = 4
LOSS_SCALE = 65536


def passed_along(value, axis, steps):
    count = lax.axis_size(axis)
    first, last = (max(0, -steps), min(count, count - steps))
    return lax.ppermute(value, axis, [(source, source + steps) for source in range(first, last)])


def doc_index(starts, positions):
    return jnp.sum((starts[None, :] <= positions[:, None]).astype(jnp.int32), axis=1) - 1


def head_block(visible, blocks):
    query_head, out_grad, key_head, value_head = blocks
    score_scale = DH ** (-0.5)
    scores = (
        jnp.einsum("tgd,kd->gtk", query_head, key_head, preferred_element_type=jnp.float32)
        * score_scale
    )
    scores = jnp.where(visible[None], scores, -1e30)
    row_max = jnp.max(scores, axis=2, keepdims=True)
    row_total = jnp.sum(jnp.exp(scores - row_max), axis=2, keepdims=True)
    prob_full = jnp.exp(scores - (row_max + jnp.log(row_total)))
    prob_low = prob_full.astype(jnp.bfloat16)
    attended = jnp.einsum("gtk,kd->tgd", prob_low, value_head, preferred_element_type=jnp.float32)
    row_delta = jnp.sum(out_grad.astype(jnp.float32) * attended, axis=2)
    d_probs = jnp.einsum("tgd,kd->gtk", out_grad, value_head, preferred_element_type=jnp.float32)
    d_scores = (prob_full * (d_probs - jnp.transpose(row_delta)[:, :, None])).astype(jnp.bfloat16)
    query_grad = (
        jnp.einsum("gtk,kd->tgd", d_scores, key_head, preferred_element_type=jnp.float32)
        * score_scale
    )
    key_grad = (
        jnp.einsum("gtk,tgd->kd", d_scores, query_head, preferred_element_type=jnp.float32)
        * score_scale
    )
    value_grad = jnp.einsum("gtk,tgd->kd", prob_low, out_grad, preferred_element_type=jnp.float32)
    return (query_grad, key_grad, value_grad)


def local(query, key_value, upstream, log_ratio, doc_starts, answer_counts):
    shard_len = query.shape[1]
    kv_width = key_value.shape[2]
    slot_count = doc_starts.shape[1]
    group_size = HQ // HK
    shard_index = lax.axis_index("ctx")
    seq_len = shard_len * lax.axis_size("ctx")
    starts = doc_starts[0]
    counts = answer_counts[0]
    doc_ends = jnp.concatenate([starts[1:], jnp.full((1,), seq_len, jnp.int32)])
    positions = shard_index * shard_len + jnp.arange(shard_len, dtype=jnp.int32)
    doc_here = doc_index(starts, positions)
    in_doc = doc_here[:, None] == jnp.arange(slot_count, dtype=jnp.int32)[None, :]
    end_here = jnp.sum(jnp.where(in_doc, doc_ends[None, :], 0), axis=1)
    count_here = jnp.sum(jnp.where(in_doc, counts[None, :], 0), axis=1)
    answer = positions >= end_here - count_here
    picked = in_doc & answer[:, None]
    partial_sum = jnp.sum(jnp.where(picked, log_ratio[0][:, None], 0.0), axis=0)
    doc_sum = lax.psum(partial_sum, "ctx")
    total_docs = lax.psum(jnp.sum((counts > 0).astype(jnp.float32)), "dp")
    floored = jnp.maximum(counts, 1).astype(jnp.float32)
    doc_coef = LOSS_SCALE * 2.0 * jax.nn.sigmoid(doc_sum / floored) / (floored * total_docs)
    weight = jnp.sum(jnp.where(picked, doc_coef[None, :], 0.0), axis=1)
    out_grad = (weight[:, None] * upstream[0].astype(jnp.float32)).astype(jnp.bfloat16)
    local_kv = key_value[0]
    earlier = [passed_along(local_kv, "ctx", distance) for distance in range(SPAN, 0, -1)]
    keys_all = jnp.concatenate(earlier + [local_kv], axis=0)
    key_pos = (shard_index - SPAN) * shard_len + jnp.arange((SPAN + 1) * shard_len, dtype=jnp.int32)
    doc_keys = doc_index(starts, key_pos)
    visible = (doc_here[:, None] == doc_keys[None, :]) & (key_pos[None, :] <= positions[:, None])
    query_heads = query[0].reshape(shard_len, HK, group_size, DH).transpose(1, 0, 2, 3)
    grad_heads = out_grad.reshape(shard_len, HK, group_size, DH).transpose(1, 0, 2, 3)
    key_heads = keys_all[:, : HK * DH].reshape(-1, HK, DH).transpose(1, 0, 2)
    value_heads = keys_all[:, HK * DH :].reshape(-1, HK, DH).transpose(1, 0, 2)
    query_grad, key_grad, value_grad = lax.map(
        partial(head_block, visible), (query_heads, grad_heads, key_heads, value_heads)
    )
    d_query = query_grad.transpose(1, 0, 2, 3).reshape(shard_len, HQ * DH).astype(jnp.bfloat16)
    kv_grad = jnp.concatenate(
        [
            key_grad.transpose(1, 0, 2).reshape(-1, HK * DH),
            value_grad.transpose(1, 0, 2).reshape(-1, HK * DH),
        ],
        axis=1,
    )
    key_pieces = kv_grad.reshape(SPAN + 1, shard_len, kv_width)
    summed = key_pieces[SPAN]
    for distance in range(1, SPAN + 1):
        summed = summed + passed_along(key_pieces[SPAN - distance], "ctx", -distance)
    return (d_query[None], summed.astype(jnp.bfloat16)[None])


def solution(mesh):
    return jax.shard_map(
        local,
        mesh=mesh,
        in_specs=(
            P("dp", "ctx", None),
            P("dp", "ctx", None),
            P("dp", "ctx", None),
            P("dp", "ctx"),
            P("dp", None),
            P("dp", None),
        ),
        out_specs=(P("dp", "ctx", None), P("dp", "ctx", None)),
        check_vma=False,
    )
```

profile of v0, /device:TPU:2, one launch (start us, length us, event | category | flops | bytes accessed | tf_op | source)
XLA Modules:
  0.0 194.1 jit_solution(14126149316577642967)
XLA Ops:
  0.6 4.2 %collective-permute-start = (bf16[192,1024]{1,0:T(8,128)(2,1)}, bf16[192,1024]{1,0:T(8,128)(2,1)}, u32[]{:S(2)}, u32[]{:S(2)}) collective-permute-start(bf16[192,1024]{1,0:T(8,128)(2,1)} %bitcast.170), channel_id=1, source_target_pairs={{0,16},{4,20},{8,24},{12,28},{1,17},{5,21},{9,25},{13,29},{2,18},{... | collective-permute-start | bytes 1179656 | tf_op jit(solution)/shard_map/ppermute | solution.py:18
  4.8 2.0 %collective-permute-start.1 = (bf16[192,1024]{1,0:T(8,128)(2,1)}, bf16[192,1024]{1,0:T(8,128)(2,1)}, u32[]{:S(2)}, u32[]{:S(2)}) collective-permute-start(bf16[192,1024]{1,0:T(8,128)(2,1)} %bitcast.171), channel_id=1, source_target_pairs={{0,12},{4,16},{8,20},{12,24},{16,28},{1,13},{5,17},{9,21},{13,25},... | collective-permute-start | bytes 1179656 | tf_op jit(solution)/shard_map/ppermute | solution.py:18
  6.9 1.9 collective-permute-start.2
  13.2 1.9 collective-permute-start.3
  15.1 16.8 %psum.14 = f32[16]{0:T(128)S(1)} all-reduce(f32[16]{0:T(128)S(1)} %select_reduce_fusion.1), channel_id=1, replica_groups=mesh['ctx'=8,'dp'=4] {'ctx'}, use_global_device_ids=true, to_apply=%region_4.5 | all-reduce | flops 16 | bytes 128 | tf_op jit(solution)/shard_map/psum | solution.py:71
  31.9 12.6 %psum.15 = f32[]{:T(128)} all-reduce(f32[]{:T(128)} %fusion.36), channel_id=1, replica_groups=mesh['ctx'=8,'dp'=4] {'dp'}, use_global_device_ids=true, to_apply=%region_6.7 | all-reduce | flops 1 | bytes 8 | tf_op jit(solution)/shard_map/psum | solution.py:72
  45.9 1.7 convert_bitcast_fusion
  48.2 1.5 fusion.29
  50.5 1.8 copy.29
  57.0 1.9 reshape.91
  60.0 60.3 %while.15 = (s32[]{:T(128)}, bf16[4,192,8,128]{3,1,2,0:T(8,128)(2,1)}, f32[4,960,128]{2,1,0:T(8,128)}, f32[4,960,128]{2,1,0:T(8,128)}, bf16[4,960,128]{2,1,0:T(8...) while((s32[]{:T(128)}, ...), condition=%wide.region_13.14_spmd.clone, body=%wide.region_9.13_spmd.clone.sunk | while | flops 2297349120 | bytes 50773160 | solution.py:87
  62.7 1.8 exponential_reduce_fusion.2
  64.5 2.7 %fusion.68 = f32[4,960,128]{2,1,0:T(8,128)} fusion(f32[4,960,128]{2,1,0:T(8,128)} %get-tuple-element.241, s32[]{:T(128)} %get-tuple-element.238, bf16[1,192,8,128]{3,2,0,1:T(8,128)(2,1)S(1)} %get-tuple-element.223, f32[960,192,8]{0,1,2:T(8,128)S(1)} %get-tuple-element.222, f32[8,192]{1,0:T(8,128)S(1)} %log_add_fusion.2, ...), kind=kOutput, calls=%fused_computation.15.clone.1 | convolution fusion | flops 383385600 | bytes 6973952 | tf_op jit(solution)/shard_map/while/body/eval_jaxpr/gtk,tgd->kd/dot_general | solution.py:49
  67.2 1.9 fusion.64
  69.2 2.4 %fusion.65 = bf16[8,192,960]{2,1,0:T(8,128)(2,1)S(1)} fusion(f32[960,192,8]{0,1,2:T(8,128)S(1)} %get-tuple-element.222, f32[8,192]{1,0:T(8,128)S(1)} %bitcast.178, f32[8,192]{1,0:T(8,128)S(1)} %log_add_fusion.2, pred[192,960]{1,0:T(8,128)(4,1)S(1)} %compare_and_fusion.2, bf16[1,192,8,128]{3,2,0,1:T(8,128)(2,1)S(1)} %get-tuple-element.223, ...), kind=kOutput, calls=%fused_computation.3.clone.1 | convolution fusion | flops 386334720 | bytes 10092548 | tf_op jit(solution)/shard_map/while/body/eval_jaxpr/tgd,kd->gtk/dot_general | solution.py:39
  71.6 1.8 fusion.67
  73.3 1.7 fusion.66
  76.4 1.4 fusion.63
  77.8 1.8 exponential_reduce_fusion.2
  79.6 2.7 %fusion.68 = f32[4,960,128]{2,1,0:T(8,128)} fusion(f32[4,960,128]{2,1,0:T(8,128)} %get-tuple-element.241, s32[]{:T(128)} %get-tuple-element.238, bf16[1,192,8,128]{3,2,0,1:T(8,128)(2,1)S(1)} %get-tuple-element.223, f32[960,192,8]{0,1,2:T(8,128)S(1)} %get-tuple-element.222, f32[8,192]{1,0:T(8,128)S(1)} %log_add_fusion.2, ...), kind=kOutput, calls=%fused_computation.15.clone.1 | convolution fusion | flops 383385600 | bytes 6973952 | tf_op jit(solution)/shard_map/while/body/eval_jaxpr/gtk,tgd->kd/dot_general | solution.py:49
  82.3 1.9 fusion.64
  84.2 2.4 %fusion.65 = bf16[8,192,960]{2,1,0:T(8,128)(2,1)S(1)} fusion(f32[960,192,8]{0,1,2:T(8,128)S(1)} %get-tuple-element.222, f32[8,192]{1,0:T(8,128)S(1)} %bitcast.178, f32[8,192]{1,0:T(8,128)S(1)} %log_add_fusion.2, pred[192,960]{1,0:T(8,128)(4,1)S(1)} %compare_and_fusion.2, bf16[1,192,8,128]{3,2,0,1:T(8,128)(2,1)S(1)} %get-tuple-element.223, ...), kind=kOutput, calls=%fused_computation.3.clone.1 | convolution fusion | flops 386334720 | bytes 10092548 | tf_op jit(solution)/shard_map/while/body/eval_jaxpr/tgd,kd->gtk/dot_general | solution.py:39
  86.6 1.8 fusion.67
  88.4 1.7 fusion.66
  92.9 1.8 exponential_reduce_fusion.2
  94.7 2.7 %fusion.68 = f32[4,960,128]{2,1,0:T(8,128)} fusion(f32[4,960,128]{2,1,0:T(8,128)} %get-tuple-element.241, s32[]{:T(128)} %get-tuple-element.238, bf16[1,192,8,128]{3,2,0,1:T(8,128)(2,1)S(1)} %get-tuple-element.223, f32[960,192,8]{0,1,2:T(8,128)S(1)} %get-tuple-element.222, f32[8,192]{1,0:T(8,128)S(1)} %log_add_fusion.2, ...), kind=kOutput, calls=%fused_computation.15.clone.1 | convolution fusion | flops 383385600 | bytes 6973952 | tf_op jit(solution)/shard_map/while/body/eval_jaxpr/gtk,tgd->kd/dot_general | solution.py:49
  97.4 1.9 fusion.64
  99.3 2.4 %fusion.65 = bf16[8,192,960]{2,1,0:T(8,128)(2,1)S(1)} fusion(f32[960,192,8]{0,1,2:T(8,128)S(1)} %get-tuple-element.222, f32[8,192]{1,0:T(8,128)S(1)} %bitcast.178, f32[8,192]{1,0:T(8,128)S(1)} %log_add_fusion.2, pred[192,960]{1,0:T(8,128)(4,1)S(1)} %compare_and_fusion.2, bf16[1,192,8,128]{3,2,0,1:T(8,128)(2,1)S(1)} %get-tuple-element.223, ...), kind=kOutput, calls=%fused_computation.3.clone.1 | convolution fusion | flops 386334720 | bytes 10092548 | tf_op jit(solution)/shard_map/while/body/eval_jaxpr/tgd,kd->gtk/dot_general | solution.py:39
  101.7 1.8 fusion.67
  103.5 1.7 fusion.66
  108.0 1.8 exponential_reduce_fusion.2
  109.8 2.7 %fusion.68 = f32[4,960,128]{2,1,0:T(8,128)} fusion(f32[4,960,128]{2,1,0:T(8,128)} %get-tuple-element.241, s32[]{:T(128)} %get-tuple-element.238, bf16[1,192,8,128]{3,2,0,1:T(8,128)(2,1)S(1)} %get-tuple-element.223, f32[960,192,8]{0,1,2:T(8,128)S(1)} %get-tuple-element.222, f32[8,192]{1,0:T(8,128)S(1)} %log_add_fusion.2, ...), kind=kOutput, calls=%fused_computation.15.clone.1 | convolution fusion | flops 383385600 | bytes 6973952 | tf_op jit(solution)/shard_map/while/body/eval_jaxpr/gtk,tgd->kd/dot_general | solution.py:49
  112.5 1.9 fusion.64
  114.4 2.4 %fusion.65 = bf16[8,192,960]{2,1,0:T(8,128)(2,1)S(1)} fusion(f32[960,192,8]{0,1,2:T(8,128)S(1)} %get-tuple-element.222, f32[8,192]{1,0:T(8,128)S(1)} %bitcast.178, f32[8,192]{1,0:T(8,128)S(1)} %log_add_fusion.2, pred[192,960]{1,0:T(8,128)(4,1)S(1)} %compare_and_fusion.2, bf16[1,192,8,128]{3,2,0,1:T(8,128)(2,1)S(1)} %get-tuple-element.223, ...), kind=kOutput, calls=%fused_computation.3.clone.1 | convolution fusion | flops 386334720 | bytes 10092548 | tf_op jit(solution)/shard_map/while/body/eval_jaxpr/tgd,kd->gtk/dot_general | solution.py:39
  116.8 1.8 fusion.67
  118.6 1.7 fusion.66
  120.4 1.9 %bitcast_dynamic-update-slice_fusion.1 = f32[960,1024]{1,0:T(8,128)S(1)} fusion(f32[4,960,128]{2,1,0:T(8,128)} %get-tuple-element.52), kind=kLoop, calls=%fused_computation.43 | loop fusion | bytes 3932160
  122.8 1.9 copy-done
  124.6 1.4 fusion.37
  126.0 1.9 collective-permute-start.4
  128.0 3.5 %collective-permute-start.5 = (f32[192,1024]{1,0:T(8,128)}, f32[192,1024]{1,0:T(8,128)}, u32[]{:S(2)}, u32[]{:S(2)}) collective-permute-start(f32[192,1024]{1,0:T(8,128)} %get-tuple-element.141), channel_id=1, source_target_pairs={{8,0},{12,4},{16,8},{20,12},{24,16},{28,20},{9,1},{13,5},{17,9},{2... | collective-permute-start | bytes 2359304 | tf_op jit(solution)/shard_map/ppermute | solution.py:18
  134.1 2.4 %copy.22 = bf16[192,4,8,128]{3,2,1,0:T(8,128)(2,1)S(1)} copy(bf16[192,4,8,128]{3,0,2,1:T(8,128)(2,1)} %bitcast.108) | data formatting | bytes 3145728 | tf_op jit(solution)/shard_map/convert_element_type | solution.py:90
  136.5 2.1 %convert_element_type.60 = bf16[1,192,4096]{2,1,0:T(8,128)(2,1)} reshape(bf16[192,4,8,128]{3,2,1,0:T(8,128)(2,1)S(1)} %copy.22) | data formatting | bytes 3145728 | tf_op jit(solution)/shard_map/convert_element_type | solution.py:90
  138.5 3.9 %collective-permute-done.4 = f32[192,1024]{1,0:T(8,128)} collective-permute-done((f32[192,1024]{1,0:T(8,128)}, f32[192,1024]{1,0:T(8,128)}, u32[]{:S(2)}, u32[]{:S(2)}) %collective-permute-start.4) | collective-permute-done | bytes 786464 | tf_op jit(solution)/shard_map/ppermute | solution.py:18
  142.5 21.1 %collective-permute-done.5 = f32[192,1024]{1,0:T(8,128)} collective-permute-done((f32[192,1024]{1,0:T(8,128)}, f32[192,1024]{1,0:T(8,128)}, u32[]{:S(2)}, u32[]{:S(2)}) %collective-permute-start.5) | collective-permute-done | bytes 786464 | tf_op jit(solution)/shard_map/ppermute | solution.py:18
  163.5 2.3 %collective-permute-done.6 = f32[192,1024]{1,0:T(8,128)} collective-permute-done((f32[192,1024]{1,0:T(8,128)S(1)}, f32[192,1024]{1,0:T(8,128)}, u32[]{:S(2)}, u32[]{:S(2)}) %collective-permute-start.6) | collective-permute-done | bytes 786464 | tf_op jit(solution)/shard_map/ppermute | solution.py:18
  165.8 25.2 %collective-permute-done.7 = f32[192,1024]{1,0:T(8,128)} collective-permute-done((f32[192,1024]{1,0:T(8,128)S(1)}, f32[192,1024]{1,0:T(8,128)}, u32[]{:S(2)}, u32[]{:S(2)}) %collective-permute-start.7) | collective-permute-done | bytes 786464 | tf_op jit(solution)/shard_map/ppermute | solution.py:18
  191.0 3.1 %fusion.34 = bf16[1,192,1024]{2,1,0:T(8,128)(2,1)} fusion(f32[192,1024]{1,0:T(8,128)} %collective-permute-done.7, f32[192,1024]{1,0:T(8,128)} %collective-permute-done.6, f32[192,1024]{1,0:T(8,128)} %collective-permute-done.5, f32[192,1024]{1,0:T(8,128)} %collective-permute-done.4, f32[960,1024]{1,0:T(8,128)} %copy-done), kind=kLoop, calls=%fused_computation.51 | loop fusion | flops 983040 | bytes 4325376 | tf_op jit(solution)/shard_map/broadcast_in_dim | solution.py:102
  (62 shorter events, 25.2 us)
Async XLA Ops:
  0.6 51.7 %collective-permute-start = (bf16[192,1024]{1,0:T(8,128)(2,1)}, bf16[192,1024]{1,0:T(8,128)(2,1)}, u32[]{:S(2)}, u32[]{:S(2)}) collective-permute-start(bf16[192,1024]{1,0:T(8,128)(2,1)} %bitcast.170), channel_id=1, source_target_pairs={{0,16},{4,20},{8,24},{12,28},{1,17},{5,21},{9,25},{13,29},{2,18},{... | collective-permute-start | bytes 1179656 | tf_op jit(solution)/shard_map/ppermute | solution.py:18
  4.8 48.5 %collective-permute-start.1 = (bf16[192,1024]{1,0:T(8,128)(2,1)}, bf16[192,1024]{1,0:T(8,128)(2,1)}, u32[]{:S(2)}, u32[]{:S(2)}) collective-permute-start(bf16[192,1024]{1,0:T(8,128)(2,1)} %bitcast.171), channel_id=1, source_target_pairs={{0,12},{4,16},{8,20},{12,24},{16,28},{1,13},{5,17},{9,21},{13,25},... | collective-permute-start | bytes 1179656 | tf_op jit(solution)/shard_map/ppermute | solution.py:18
  6.9 47.5 %collective-permute-start.2 = (bf16[192,1024]{1,0:T(8,128)(2,1)}, bf16[192,1024]{1,0:T(8,128)(2,1)S(1)}, u32[]{:S(2)}, u32[]{:S(2)}) collective-permute-start(bf16[192,1024]{1,0:T(8,128)(2,1)} %bitcast.172), channel_id=1, source_target_pairs={{0,8},{4,12},{8,16},{12,20},{16,24},{20,28},{1,9},{5,13},{9,17},{1... | collective-permute-start | bytes 1179656 | tf_op jit(solution)/shard_map/ppermute | solution.py:18
  13.2 41.2 %collective-permute-start.3 = (bf16[192,1024]{1,0:T(8,128)(2,1)}, bf16[192,1024]{1,0:T(8,128)(2,1)}, u32[]{:S(2)}, u32[]{:S(2)}) collective-permute-start(bf16[192,1024]{1,0:T(8,128)(2,1)} %bitcast.173), channel_id=1, source_target_pairs={{0,4},{4,8},{8,12},{12,16},{16,20},{20,24},{24,28},{1,5},{5,9},{9,... | collective-permute-start | bytes 1179656 | tf_op jit(solution)/shard_map/ppermute | solution.py:18
  50.5 5.0 %copy-start.3 = (bf16[1,192,1024]{2,1,0:T(8,128)(2,1)S(1)}, bf16[1,192,1024]{2,1,0:T(8,128)(2,1)}, u32[]{:S(2)}) copy-start(bf16[1,192,1024]{2,1,0:T(8,128)(2,1)} %param.9) | copy-start | bytes 1179652
  64.5 2.7 %copy-start.2 = (bf16[4,960,128]{2,1,0:T(8,128)(2,1)S(1)}, bf16[4,960,128]{2,1,0:T(8,128)(2,1)}, u32[]{:S(2)}) copy-start(bf16[4,960,128]{2,1,0:T(8,128)(2,1)} %get-tuple-element.257) | copy-start | bytes 2949124 | tf_op jit(solution)/shard_map/while
  79.6 2.7 %copy-start.2 = (bf16[4,960,128]{2,1,0:T(8,128)(2,1)S(1)}, bf16[4,960,128]{2,1,0:T(8,128)(2,1)}, u32[]{:S(2)}) copy-start(bf16[4,960,128]{2,1,0:T(8,128)(2,1)} %get-tuple-element.257) | copy-start | bytes 2949124 | tf_op jit(solution)/shard_map/while
  94.7 2.7 %copy-start.2 = (bf16[4,960,128]{2,1,0:T(8,128)(2,1)S(1)}, bf16[4,960,128]{2,1,0:T(8,128)(2,1)}, u32[]{:S(2)}) copy-start(bf16[4,960,128]{2,1,0:T(8,128)(2,1)} %get-tuple-element.257) | copy-start | bytes 2949124 | tf_op jit(solution)/shard_map/while
  109.8 2.7 %copy-start.2 = (bf16[4,960,128]{2,1,0:T(8,128)(2,1)S(1)}, bf16[4,960,128]{2,1,0:T(8,128)(2,1)}, u32[]{:S(2)}) copy-start(bf16[4,960,128]{2,1,0:T(8,128)(2,1)} %get-tuple-element.257) | copy-start | bytes 2949124 | tf_op jit(solution)/shard_map/while
  120.4 2.1 %copy-start.1 = (f32[4,960,128]{2,1,0:T(8,128)S(1)}, f32[4,960,128]{2,1,0:T(8,128)}, u32[]{:S(2)}) copy-start(f32[4,960,128]{2,1,0:T(8,128)} %get-tuple-element.53) | copy-start | bytes 5898244
  122.8 1.9 copy-start
  126.0 16.4 %collective-permute-start.4 = (f32[192,1024]{1,0:T(8,128)}, f32[192,1024]{1,0:T(8,128)}, u32[]{:S(2)}, u32[]{:S(2)}) collective-permute-start(f32[192,1024]{1,0:T(8,128)} %get-tuple-element.138), channel_id=1, source_target_pairs={{4,0},{8,4},{12,8},{16,12},{20,16},{24,20},{28,24},{5,1},{9,5},{13... | collective-permute-start | bytes 2359304 | tf_op jit(solution)/shard_map/ppermute | solution.py:18
  128.0 35.6 %collective-permute-start.5 = (f32[192,1024]{1,0:T(8,128)}, f32[192,1024]{1,0:T(8,128)}, u32[]{:S(2)}, u32[]{:S(2)}) collective-permute-start(f32[192,1024]{1,0:T(8,128)} %get-tuple-element.141), channel_id=1, source_target_pairs={{8,0},{12,4},{16,8},{20,12},{24,16},{28,20},{9,1},{13,5},{17,9},{2... | collective-permute-start | bytes 2359304 | tf_op jit(solution)/shard_map/ppermute | solution.py:18
  131.5 34.3 %collective-permute-start.6 = (f32[192,1024]{1,0:T(8,128)S(1)}, f32[192,1024]{1,0:T(8,128)}, u32[]{:S(2)}, u32[]{:S(2)}) collective-permute-start(f32[192,1024]{1,0:T(8,128)S(1)} %get-tuple-element.140), channel_id=1, source_target_pairs={{12,0},{16,4},{20,8},{24,12},{28,16},{13,1},{17,5},{21,9},{25,13},... | collective-permute-start | bytes 2359304 | tf_op jit(solution)/shard_map/ppermute | solution.py:18
  132.8 58.2 %collective-permute-start.7 = (f32[192,1024]{1,0:T(8,128)S(1)}, f32[192,1024]{1,0:T(8,128)}, u32[]{:S(2)}, u32[]{:S(2)}) collective-permute-start(f32[192,1024]{1,0:T(8,128)S(1)} %get-tuple-element.139), channel_id=1, source_target_pairs={{16,0},{20,4},{24,8},{28,12},{17,1},{21,5},{25,9},{29,13},{18,2},{... | collective-permute-start | bytes 2359304 | tf_op jit(solution)/shard_map/ppermute | solution.py:18
where the time goes:
time: 195 us; the launch traced here: 194 us
  waiting for transfers between devices  52.4 us (27%)
  matrix products  47.7 us (24%)
  blocking collectives  29.4 us (15%)
  local copies, waits for them, and re-layouts  25.2 us (13%)
  other arithmetic  20.3 us (10%)
  starting transfers between devices  18.1 us (9%)
    ppermute x8, waiting for transfers between devices, passed_along(): lax.ppermute(value, axis, [(source, source + steps) for source in range(f...  52.4 us
    ppermute x8, starting transfers between devices, passed_along(): lax.ppermute(value, axis, [(source, source + steps) for source in range(f...  18.1 us
    psum x1, blocking collectives, local(): doc_sum = lax.psum(partial_sum, 'ctx')  16.8 us
    psum x1, blocking collectives, local(): total_docs = lax.psum(jnp.sum((counts > 0).astype(jnp.float32)), 'dp')  12.6 us
    dot_general x4, matrix products, head_block(): jnp.einsum('gtk,tgd->kd', prob_low, out_grad, preferred_element_type=jnp....  10.8 us
    unnamed x15, local copies, waits for them, and re-layouts  10.7 us
    dot_general x4, matrix products, head_block(): jnp.einsum('tgd,kd->gtk', out_grad, value_head, preferred_element_type=jn...  9.61 us
    dot_general x4, matrix products, head_block(): jnp.einsum('gtk,kd->tgd', prob_low, value_head, preferred_element_type=jn...  7.65 us
  transfers between devices with their start and end apart: 8, of which 4 were waited for; matrix products, arithmetic and copies ran while one was open for 10% of the time, Pallas kernels for 0%

commit v1 on v0

v1 whole, which is shorter than its diff:
```python
from functools import partial

import jax
import jax.numpy as jnp
from jax import lax
from jax.experimental import pallas as pl
from jax.experimental.pallas import tpu as pltpu
from jax.sharding import PartitionSpec as P

HQ = 32
HK = 4
DH = 128
SPAN = 4
LOSS_SCALE = 65536
PAIR = 2
MESH_ID = pl.DeviceIdType.MESH
LOG2E = 1.4426950408889634


def as_column(row, shift=0):
    size = row.shape[1]
    r = lax.broadcasted_iota(jnp.int32, (size, size), 0)
    c = lax.broadcasted_iota(jnp.int32, (size, size), 1)
    return jnp.sum(jnp.where(c == r + shift, row, 0.0), axis=1, keepdims=True)


def dot_nt(a, b):
    return lax.dot_general(a, b, (((1,), (1,)), ((), ())), preferred_element_type=jnp.float32)


def kernel(
    n_ctx, n_dp,
    q_ref, kv_ref, up_ref, lr_ref, st_ref, ct_ref,
    dq_ref, dkv_ref,
    kv_all, kt_buf, bias, wcol_ref, acc, gown, gsend, grecv, psend, precv, dsend, drecv,
    kv_ss, kv_rs, g_ss, g_rs, p_ss, p_rs, d_ss, d_rs,
):
    tok = q_ref.shape[0]
    slots = st_ref.shape[1]
    group = HQ // HK
    width = PAIR * tok
    me = lax.axis_index("ctx")
    my_dp = lax.axis_index("dp")
    seq_len = n_ctx * tok
    scale = DH ** (-0.5)

    precv[...] = jnp.zeros_like(precv)

    barrier = pltpu.get_barrier_semaphore()
    for d in range(1, SPAN + 1):
        @pl.when(me + d < n_ctx)
        def _():
            pl.semaphore_signal(barrier, inc=1, device_id={"ctx": me + d}, device_id_type=MESH_ID)

        @pl.when(me >= d)
        def _():
            pl.semaphore_signal(barrier, inc=1, device_id={"ctx": me - d}, device_id_type=MESH_ID)
    for k in range(1, n_dp):
        pl.semaphore_signal(
            barrier, inc=1, device_id={"dp": lax.rem(my_dp + k, n_dp)}, device_id_type=MESH_ID
        )

    for g in range(HK):
        kv_all[g, SPAN * tok:, 0:DH] = kv_ref[:, g * DH:(g + 1) * DH]
        kv_all[g, SPAN * tok:, DH:2 * DH] = kv_ref[:, (HK + g) * DH:(HK + g + 1) * DH]
    for d in range(1, SPAN + 1):
        @pl.when(me < d)
        def _():
            lo = (SPAN - d) * tok
            kv_all[:, lo:lo + tok, :] = jnp.zeros((HK, tok, 2 * DH), jnp.bfloat16)

    starts = as_column(st_ref[...].astype(jnp.float32))
    slot_col = lax.broadcasted_iota(jnp.int32, (slots, 1), 0)
    ends = as_column(st_ref[...].astype(jnp.float32), 1)
    ends = ends + jnp.where(slot_col == slots - 1, jnp.float32(seq_len), 0.0)
    counts_row = ct_ref[...].astype(jnp.float32)
    counts = as_column(counts_row)
    lane = lax.broadcasted_iota(jnp.int32, (1, width), 1)
    pos = (me * tok + jnp.where(lane >= tok, lane - tok, lane)).astype(jnp.float32)
    in_doc = (pos >= starts) & (pos < ends)
    picked = (in_doc & (pos >= ends - counts)).astype(jnp.float32)
    part = jnp.sum(picked[:, :tok] * lr_ref[...], axis=1, keepdims=True)
    psend[...] = jnp.broadcast_to(part, (slots, 128))
    docs = jnp.sum((counts_row > 0).astype(jnp.float32), axis=1, keepdims=True)
    dsend[...] = jnp.broadcast_to(docs, (8, 128))

    pl.semaphore_wait(
        barrier, jnp.minimum(me, SPAN) + jnp.minimum(n_ctx - 1 - me, SPAN) + (n_dp - 1)
    )

    def part_copy(e):
        return pltpu.make_async_remote_copy(
            src_ref=psend, dst_ref=precv.at[SPAN - e],
            send_sem=p_ss.at[SPAN - e], recv_sem=p_rs.at[SPAN - e],
            device_id={"ctx": me + e}, device_id_type=MESH_ID,
        )

    def docs_copy(k):
        return pltpu.make_async_remote_copy(
            src_ref=dsend, dst_ref=drecv.at[k - 1],
            send_sem=d_ss.at[k - 1], recv_sem=d_rs.at[k - 1],
            device_id={"dp": lax.rem(my_dp + k, n_dp)}, device_id_type=MESH_ID,
        )

    def kv_copy(g, d):
        return pltpu.make_async_remote_copy(
            src_ref=kv_all.at[g, pl.ds(SPAN * tok, tok), :],
            dst_ref=kv_all.at[g, pl.ds((SPAN - d) * tok, tok), :],
            send_sem=kv_ss.at[g, SPAN - d], recv_sem=kv_rs.at[g, SPAN - d],
            device_id={"ctx": me + d}, device_id_type=MESH_ID,
        )

    def grad_copy(g, d):
        return pltpu.make_async_remote_copy(
            src_ref=gsend.at[g, SPAN - d], dst_ref=grecv.at[g, SPAN - d],
            send_sem=g_ss.at[g, SPAN - d], recv_sem=g_rs.at[g, SPAN - d],
            device_id={"ctx": me - d}, device_id_type=MESH_ID,
        )

    def can_send(e):
        return me + e < n_ctx if e > 0 else me + e >= 0

    offsets = [e for e in range(-SPAN, SPAN + 1) if e != 0]
    for e in offsets:
        @pl.when(can_send(e))
        def _():
            part_copy(e).start()
    for k in range(1, n_dp):
        docs_copy(k).start()
    for g in range(HK):
        for d in range(1, SPAN + 1):
            @pl.when(me + d < n_ctx)
            def _():
                kv_copy(g, d).start()

    doc_lo = jnp.sum(jnp.where(in_doc, starts, 0.0), axis=0, keepdims=True)
    kpos = (
        (me - SPAN) * tok + lax.broadcasted_iota(jnp.int32, ((SPAN + 1) * tok, 1), 0)
    ).astype(jnp.float32)
    bias[...] = jnp.where((kpos >= doc_lo) & (kpos <= pos), 0.0, -1e30)

    for e in offsets:
        @pl.when(can_send(-e))
        def _():
            part_copy(e).wait_recv()
    for k in range(1, n_dp):
        docs_copy(k).wait_recv()
    doc_sum = psend[...]
    for e in offsets:
        doc_sum = doc_sum + precv[SPAN - e]
    doc_sum = doc_sum[:, 0:1]
    total = dsend[...]
    for k in range(1, n_dp):
        total = total + drecv[k - 1]
    floored = jnp.maximum(counts, 1.0)
    prob = 1.0 / (1.0 + jnp.exp(-(doc_sum / floored)))
    coef = LOSS_SCALE * 2.0 * prob / (floored * total[0:1, 0:1])
    weight = jnp.sum(picked[:, :tok] * coef, axis=0, keepdims=True)
    wcol_ref[...] = jnp.broadcast_to(as_column(weight), (tok, 128))

    def one_group(g, carry):
        for d in range(1, SPAN + 1):
            @pl.when(me >= d)
            def _():
                kv_copy(g, d).wait_recv()
        kt_buf[...] = kv_all[g, :, 0:DH].T
        acc[...] = jnp.zeros_like(acc)

        def one_pair(j, carry):
            first = (g * group + j * PAIR) * DH
            cols = [pl.ds(pl.multiple_of(first + i * DH, DH), DH) for i in range(PAIR)]
            keys = kv_all[g, :, 0:DH]
            vals = kv_all[g, :, DH:2 * DH]
            q2 = jnp.concatenate([q_ref[:, c] for c in cols], axis=0)
            wcol = wcol_ref[...]
            og2 = jnp.concatenate(
                [(wcol * up_ref[:, c].astype(jnp.float32)).astype(jnp.bfloat16) for c in cols],
                axis=0,
            )
            s = dot_nt(keys, q2) * (scale * LOG2E) + bias[...]
            e = jnp.exp2(s - jnp.max(s, axis=0, keepdims=True))
            inv = 1.0 / jnp.sum(e, axis=0, keepdims=True)
            p = e * inv
            dp = dot_nt(vals, og2)
            delta = jnp.sum(p * dp, axis=0, keepdims=True)
            p_low = p.astype(jnp.bfloat16)
            ds = (p * (dp - delta)).astype(jnp.bfloat16)
            dqt = jnp.dot(kt_buf[...], ds, preferred_element_type=jnp.float32) * scale
            dq = dqt.T.astype(jnp.bfloat16)
            for i, c in enumerate(cols):
                dq_ref[:, c] = dq[i * tok:(i + 1) * tok]
            acc[:, 0:DH] += jnp.dot(ds, q2, preferred_element_type=jnp.float32)
            acc[:, DH:2 * DH] += jnp.dot(p_low, og2, preferred_element_type=jnp.float32)
            return carry

        lax.fori_loop(0, group // PAIR, one_pair, 0)
        acc[:, 0:DH] = acc[:, 0:DH] * scale
        for d in range(1, SPAN + 1):
            lo = (SPAN - d) * tok
            @pl.when(me >= d)
            def _():
                gsend[g, SPAN - d] = acc[lo:lo + tok, :].astype(jnp.bfloat16)
                grad_copy(g, d).start()
        gown[g] = acc[SPAN * tok:, :]
        return carry

    lax.fori_loop(0, HK, one_group, 0)

    for g in range(HK):
        for d in range(1, SPAN + 1):
            @pl.when(me + d < n_ctx)
            def _():
                grad_copy(g, d).wait_recv()
                gown[g] += grecv[g, SPAN - d].astype(jnp.float32)
        out = gown[g].astype(jnp.bfloat16)
        dkv_ref[:, g * DH:(g + 1) * DH] = out[:, 0:DH]
        dkv_ref[:, (HK + g) * DH:(HK + g + 1) * DH] = out[:, DH:2 * DH]

    for e in offsets:
        @pl.when(can_send(e))
        def _():
            part_copy(e).wait_send()
    for k in range(1, n_dp):
        docs_copy(k).wait_send()
    for g in range(HK):
        for d in range(1, SPAN + 1):
            @pl.when(me + d < n_ctx)
            def _():
                kv_copy(g, d).wait_send()

            @pl.when(me >= d)
            def _():
                grad_copy(g, d).wait_send()


def local(n_ctx, n_dp, query, key_value, upstream, log_ratio, doc_starts, answer_counts):
    tok = query.shape[1]
    slots = doc_starts.shape[1]
    window = (SPAN + 1) * tok
    f32, bf16 = jnp.float32, jnp.bfloat16
    sem = pltpu.SemaphoreType.DMA
    vmem = pl.BlockSpec(memory_space=pltpu.VMEM)
    flops = 10 * HQ * tok * window * DH
    d_query, d_kv = pl.pallas_call(
        partial(kernel, n_ctx, n_dp),
        out_shape=(
            jax.ShapeDtypeStruct(query.shape[1:], bf16),
            jax.ShapeDtypeStruct(key_value.shape[1:], bf16),
        ),
        in_specs=[vmem] * 6,
        out_specs=(vmem, vmem),
        scratch_shapes=[
            pltpu.VMEM((HK, window, 2 * DH), bf16),
            pltpu.VMEM((DH, window), bf16),
            pltpu.VMEM((window, PAIR * tok), f32),
            pltpu.VMEM((tok, 128), f32),
            pltpu.VMEM((window, 2 * DH), f32),
            pltpu.VMEM((HK, tok, 2 * DH), f32),
            pltpu.VMEM((HK, SPAN, tok, 2 * DH), bf16),
            pltpu.VMEM((HK, SPAN, tok, 2 * DH), bf16),
            pltpu.VMEM((slots, 128), f32),
            pltpu.VMEM((2 * SPAN + 1, slots, 128), f32),
            pltpu.VMEM((8, 128), f32),
            pltpu.VMEM((max(n_dp - 1, 1), 8, 128), f32),
            sem((HK, SPAN)), sem((HK, SPAN)), sem((HK, SPAN)), sem((HK, SPAN)),
            sem((2 * SPAN + 1,)), sem((2 * SPAN + 1,)),
            sem((max(n_dp - 1, 1),)), sem((max(n_dp - 1, 1),)),
        ],
        compiler_params=pltpu.CompilerParams(
            collective_id=0, has_side_effects=True, vmem_limit_bytes=48 * 1024 * 1024
        ),
        cost_estimate=pl.CostEstimate(
            flops=flops, bytes_accessed=8 * 1024 * 1024, transcendentals=HQ * tok * window
        ),
    )(query[0], key_value[0], upstream[0], log_ratio, doc_starts, answer_counts)
    return (d_query[None], d_kv[None])


def solution(mesh):
    n_ctx, n_dp = mesh.shape["ctx"], mesh.shape["dp"]
    return jax.shard_map(
        partial(local, n_ctx, n_dp),
        mesh=mesh,
        in_specs=(
            P("dp", "ctx", None),
            P("dp", "ctx", None),
            P("dp", "ctx", None),
            P("dp", "ctx"),
            P("dp", None),
            P("dp", None),
        ),
        out_specs=(P("dp", "ctx", None), P("dp", "ctx", None)),
        check_vma=False,
    )
```

time: 195 us -> 68.7 us (0.35)
  Pallas kernels: 0 us -> 59.7 us
  waiting for transfers between devices: 52.4 us -> 0 us
  matrix products: 47.7 us -> 0 us
  blocking collectives: 29.4 us -> 0 us
  other arithmetic: 20.3 us -> 0 us
  starting transfers between devices: 18.1 us -> 0 us
  local copies, waits for them, and re-layouts: 25.2 us -> 7.68 us
    pallas_call x0 -> x1, Pallas kernels: none -> 59.7 us  [local(): pl.pallas_call(partial(kernel, n_ctx, n_dp), out_shape=(jax.ShapeDtypeStr...]
    ppermute x8 -> x0, waiting for transfers between devices: 52.4 us -> none  [passed_along(): lax.ppermute(value, axis, [(source, source + steps) for source in range(f...]
    dot_general x24 -> x0, matrix products: 47.7 us -> none  [the longest x4 10.8 us: head_block(): jnp.einsum('gtk,tgd->kd', prob_low, out_grad, preferred_element_type=jnp....]
    psum x2 -> x0, blocking collectives: 29.4 us -> none  [the longest x1 16.8 us: local(): doc_sum = lax.psum(partial_sum, 'ctx')]
    ppermute x8 -> x0, starting transfers between devices: 18.1 us -> none  [passed_along(): lax.ppermute(value, axis, [(source, source + steps) for source in range(f...]
    reduce_sum x10 -> x0, other arithmetic: 11.6 us -> none  [the longest x4 7.22 us: head_block(): row_total = jnp.sum(jnp.exp(scores - row_max), axis=2, keepdims=True)]
    convert_element_type x2 -> x0, local copies, waits for them, and re-layouts: 4.48 us -> none  [local(): query_grad.transpose(1, 0, 2, 3).reshape(shard_len, HQ * DH)]
    dynamic_slice x4 -> x0, local copies, waits for them, and re-layouts: 4.29 us -> none  [local(): lax.map(partial(head_block, visible), (query_heads, grad_heads, key_heads...]
  transfers between devices with their start and end apart: 8 -> 0, of which waited for: 4 -> 0; matrix products, arithmetic and copies ran while one was open for 10% -> 0% of each run, Pallas kernels for 0% -> 0%
where the time goes in v1:
time: 68.7 us; the launch traced here: 68 us
  Pallas kernels  59.7 us (87%)
  local copies, waits for them, and re-layouts  7.68 us (11%)
    pallas_call x1, Pallas kernels, local(): pl.pallas_call(partial(kernel, n_ctx, n_dp), out_shape=(jax.ShapeDtypeStr...  59.7 us
    unnamed x14, local copies, waits for them, and re-layouts  7.68 us

profile of v1, /device:TPU:2, one launch (start us, length us, event | category | flops | bytes accessed | tf_op | source)
XLA Modules:
  0.0 68.0 jit_solution(11223380787459175789)
XLA Ops:
  0.6 0.0 copy-start
  0.6 1.4 %copy-done = bf16[1,192,4096]{2,1,0:T(8,128)(2,1)S(1)} copy-done((bf16[1,192,4096]{2,1,0:T(8,128)(2,1)S(1)}, bf16[1,192,4096]{2,1,0:T(8,128)(2,1)}, u32[]{:S(2)}) %copy-start) | copy-done | bytes 1572888
  2.0 0.0 copy-start.1
  2.0 1.4 %copy-done.1 = bf16[1,192,4096]{2,1,0:T(8,128)(2,1)S(1)} copy-done((bf16[1,192,4096]{2,1,0:T(8,128)(2,1)S(1)}, bf16[1,192,4096]{2,1,0:T(8,128)(2,1)}, u32[]{:S(2)}) %copy-start.1) | copy-done | bytes 1572888
  3.4 0.0 copy-start.2
  3.5 1.0 %copy-done.2 = bf16[1,192,1024]{2,1,0:T(8,128)(2,1)S(1)} copy-done((bf16[1,192,1024]{2,1,0:T(8,128)(2,1)S(1)}, bf16[1,192,1024]{2,1,0:T(8,128)(2,1)}, u32[]{:S(2)}) %copy-start.2) | copy-done | bytes 393240
  4.4 0.0 copy-start.3
  4.4 0.7 copy-done.3
  5.1 0.0 copy-start.4
  5.1 0.7 copy-done.4
  5.8 0.0 copy-start.5
  5.8 0.7 copy-done.5
  6.4 59.7 %shard_map.77 = (bf16[192,4096]{1,0:T(8,128)(2,1)S(1)}, bf16[192,1024]{1,0:T(8,128)(2,1)S(1)}) custom-call(bf16[192,4096]{1,0:T(8,128)(2,1)S(1)} %bitcast.7, bf16[192,1024]{1,0:T(8,128)(2,1)S(1)} %bitcast.9, bf16[192,4096]{1,0:T(8,128)(2,1)S(1)} %bitcast.8, f32[1,192]{1,0:T(1,128)S(1)} %copy-done.3, s32[1,16]{1,0:T(1,128)S(1)} %copy-done.4, ...), custom_call_target="tpu_custom_call" | custom-call | flops 7549747200 | bytes 8388608 | tf_op jit(solution)/shard_map/pallas_call | solution.py:244
  66.1 1.1 %copy.10 = bf16[1,192,4096]{2,1,0:T(8,128)(2,1)} copy(bf16[1,192,4096]{2,1,0:T(8,128)(2,1)S(1)} %bitcast.5) | data formatting | bytes 3145728
  67.3 0.7 %copy.11 = bf16[1,192,1024]{2,1,0:T(8,128)(2,1)} copy(bf16[1,192,1024]{2,1,0:T(8,128)(2,1)S(1)} %bitcast.6) | data formatting | bytes 786432
Async XLA Ops:
  0.6 1.4 %copy-start = (bf16[1,192,4096]{2,1,0:T(8,128)(2,1)S(1)}, bf16[1,192,4096]{2,1,0:T(8,128)(2,1)}, u32[]{:S(2)}) copy-start(bf16[1,192,4096]{2,1,0:T(8,128)(2,1)} %param.6) | copy-start | bytes 4718596
  2.0 1.4 %copy-start.1 = (bf16[1,192,4096]{2,1,0:T(8,128)(2,1)S(1)}, bf16[1,192,4096]{2,1,0:T(8,128)(2,1)}, u32[]{:S(2)}) copy-start(bf16[1,192,4096]{2,1,0:T(8,128)(2,1)} %param.8) | copy-start | bytes 4718596
  3.4 1.0 %copy-start.2 = (bf16[1,192,1024]{2,1,0:T(8,128)(2,1)S(1)}, bf16[1,192,1024]{2,1,0:T(8,128)(2,1)}, u32[]{:S(2)}) copy-start(bf16[1,192,1024]{2,1,0:T(8,128)(2,1)} %param.7) | copy-start | bytes 1179652
  4.4 0.7 copy-start.3
  5.1 0.7 copy-start.4
  5.8 0.7 copy-start.5

commit v2 on v1

--- a/solution.py
+++ b/solution.py
@@ -30,10 +30,12 @@
 
 def kernel(
     n_ctx, n_dp,
-    q_ref, kv_ref, up_ref, lr_ref, st_ref, ct_ref,
+    q_hbm, kv_hbm, up_hbm, lr_hbm, st_hbm, ct_hbm,
     dq_ref, dkv_ref,
-    kv_all, kt_buf, bias, wcol_ref, acc, gown, gsend, grecv, psend, precv, dsend, drecv,
-    kv_ss, kv_rs, g_ss, g_rs, p_ss, p_rs, d_ss, d_rs,
+    q_ref, up_ref, lr_ref, st_ref, ct_ref,
+    kv_all, kt_buf, bias, wcol_ref, acc, gown, gsend, xrecv, csend, grecv,
+    psend, precv, dsend, drecv,
+    in_s, kv_ss, kv_rs, x_ss, x_rs, g_ss, g_rs, p_ss, p_rs, d_ss, d_rs,
 ):
     tok = q_ref.shape[0]
     slots = st_ref.shape[1]
@@ -41,8 +43,38 @@
     width = PAIR * tok
     me = lax.axis_index("ctx")
     my_dp = lax.axis_index("dp")
+    parity = lax.rem(me, 2)
+    even = parity == 0
+    odd = parity == 1
+    partner = me + 1 - 2 * parity
     seq_len = n_ctx * tok
     scale = DH ** (-0.5)
+
+    def small_in():
+        pairs = ((st_hbm, st_ref), (ct_hbm, ct_ref), (lr_hbm, lr_ref))
+        return [pltpu.make_async_copy(a, b, in_s.at[i]) for i, (a, b) in enumerate(pairs)]
+
+    def kv_in():
+        copies = []
+        for g in range(HK):
+            for i in range(2):
+                copies.append(
+                    pltpu.make_async_copy(
+                        kv_hbm.at[:, pl.ds((i * HK + g) * DH, DH)],
+                        kv_all.at[g, pl.ds(SPAN * tok, tok), pl.ds(i * DH, DH)],
+                        in_s.at[5 + 2 * g + i],
+                    )
+                )
+        return copies
+
+    def big_in():
+        return [
+            pltpu.make_async_copy(q_hbm, q_ref, in_s.at[3]),
+            pltpu.make_async_copy(up_hbm, up_ref, in_s.at[4]),
+        ]
+
+    for c in small_in() + kv_in() + big_in():
+        c.start()
 
     precv[...] = jnp.zeros_like(precv)
 
@@ -60,15 +92,100 @@
             barrier, inc=1, device_id={"dp": lax.rem(my_dp + k, n_dp)}, device_id_type=MESH_ID
         )
 
-    for g in range(HK):
-        kv_all[g, SPAN * tok:, 0:DH] = kv_ref[:, g * DH:(g + 1) * DH]
-        kv_all[g, SPAN * tok:, DH:2 * DH] = kv_ref[:, (HK + g) * DH:(HK + g + 1) * DH]
     for d in range(1, SPAN + 1):
         @pl.when(me < d)
         def _():
             lo = (SPAN - d) * tok
             kv_all[:, lo:lo + tok, :] = jnp.zeros((HK, tok, 2 * DH), jnp.bfloat16)
 
+    def remote(src, dst, ss, rs, ctx):
+        return pltpu.make_async_remote_copy(
+            src_ref=src, dst_ref=dst, send_sem=ss, recv_sem=rs,
+            device_id={"ctx": ctx}, device_id_type=MESH_ID,
+        )
+
+    def part_copy(e):
+        return remote(psend, precv.at[SPAN - e], p_ss.at[SPAN - e], p_rs.at[SPAN - e], me + e)
+
+    def docs_copy(k):
+        return pltpu.make_async_remote_copy(
+            src_ref=dsend, dst_ref=drecv.at[k - 1],
+            send_sem=d_ss.at[k - 1], recv_sem=d_rs.at[k - 1],
+            device_id={"dp": lax.rem(my_dp + k, n_dp)}, device_id_type=MESH_ID,
+        )
+
+    def kv_slot(g, d):
+        return kv_all.at[g, pl.ds((SPAN - d) * tok, tok), :]
+
+    def kv_copy(g, source, dest, index, ctx):
+        return remote(
+            kv_slot(g, source), kv_slot(g, dest), kv_ss.at[g, index], kv_rs.at[g, SPAN - dest], ctx
+        )
+
+    def kv_sends(g):
+        return [
+            (me + 2 < n_ctx, kv_copy(g, 0, 2, 0, me + 2)),
+            (me + 4 < n_ctx, kv_copy(g, 0, 4, 1, me + 4)),
+            (even, kv_copy(g, 0, 1, 2, partner)),
+        ]
+
+    def kv_forwards(g):
+        return [
+            (2, even & (me >= 2), kv_copy(g, 2, 3, 3, partner)),
+            (2, odd & (me >= 2), kv_copy(g, 2, 1, 3, partner)),
+            (4, odd & (me >= 4), kv_copy(g, 4, 3, 4, partner)),
+        ]
+
+    def kv_wait(g, d):
+        @pl.when(me >= d)
+        def _():
+            kv_copy(g, 0, d, 0, partner).wait_recv()
+
+    def forward(g):
+        for d in (2, 4):
+            kv_wait(g, d)
+            for source, cond, copy in kv_forwards(g):
+                if source == d:
+                    pl.when(cond)(copy.start)
+
+    def exchange_copies(g):
+        return [
+            (even & (me >= 2), remote(gsend.at[g, SPAN - 1], xrecv.at[g, 0], x_ss.at[g, 0], x_rs.at[g, 0], partner)),
+            (even & (me >= 2), remote(gsend.at[g, SPAN - 2], xrecv.at[g, 1], x_ss.at[g, 1], x_rs.at[g, 1], partner)),
+            (odd & (me >= 4), remote(gsend.at[g, SPAN - 4], xrecv.at[g, 0], x_ss.at[g, 0], x_rs.at[g, 0], partner)),
+            (odd, remote(gsend.at[g, SPAN - 1], grecv.at[g, 0], g_ss.at[g, 0], g_rs.at[g, 0], partner)),
+            (even & (me >= 4), remote(gsend.at[g, SPAN - 4], grecv.at[g, 2], g_ss.at[g, 0], g_rs.at[g, 2], me - 4)),
+        ]
+
+    def final_copies(g):
+        return [
+            (even & (me >= 4), remote(csend.at[g, 0], grecv.at[g, 2], g_ss.at[g, 1], g_rs.at[g, 2], me - 3)),
+            (odd & (me >= 2), remote(csend.at[g, 0], grecv.at[g, 1], g_ss.at[g, 1], g_rs.at[g, 1], me - 2)),
+            (odd & (me >= 2), remote(csend.at[g, 1], grecv.at[g, 1], g_ss.at[g, 2], g_rs.at[g, 1], me - 3)),
+        ]
+
+    def combine(g):
+        def add(i, d):
+            both = gsend[g, SPAN - d].astype(jnp.float32) + xrecv[g, i].astype(jnp.float32)
+            csend[g, i] = both.astype(jnp.bfloat16)
+
+        @pl.when(even & (me >= 4))
+        def _():
+            exchange_copies(g)[2][1].wait_recv()
+            add(0, 3)
+            final_copies(g)[0][1].start()
+
+        @pl.when(odd & (me >= 2))
+        def _():
+            exchange_copies(g)[0][1].wait_recv()
+            add(0, 2)
+            final_copies(g)[1][1].start()
+            exchange_copies(g)[1][1].wait_recv()
+            add(1, 3)
+            final_copies(g)[2][1].start()
+
+    for c in small_in():
+        c.wait()
     starts = as_column(st_ref[...].astype(jnp.float32))
     slot_col = lax.broadcasted_iota(jnp.int32, (slots, 1), 0)
     ends = as_column(st_ref[...].astype(jnp.float32), 1)
@@ -83,40 +200,13 @@
     psend[...] = jnp.broadcast_to(part, (slots, 128))
     docs = jnp.sum((counts_row > 0).astype(jnp.float32), axis=1, keepdims=True)
     dsend[...] = jnp.broadcast_to(docs, (8, 128))
+    for c in kv_in():
+        c.wait()
 
     pl.semaphore_wait(
         barrier, jnp.minimum(me, SPAN) + jnp.minimum(n_ctx - 1 - me, SPAN) + (n_dp - 1)
     )
 
-    def part_copy(e):
-        return pltpu.make_async_remote_copy(
-            src_ref=psend, dst_ref=precv.at[SPAN - e],
-            send_sem=p_ss.at[SPAN - e], recv_sem=p_rs.at[SPAN - e],
-            device_id={"ctx": me + e}, device_id_type=MESH_ID,
-        )
-
-    def docs_copy(k):
-        return pltpu.make_async_remote_copy(
-            src_ref=dsend, dst_ref=drecv.at[k - 1],
-            send_sem=d_ss.at[k - 1], recv_sem=d_rs.at[k - 1],
-            device_id={"dp": lax.rem(my_dp + k, n_dp)}, device_id_type=MESH_ID,
-        )
-
-    def kv_copy(g, d):
-        return pltpu.make_async_remote_copy(
-            src_ref=kv_all.at[g, pl.ds(SPAN * tok, tok), :],
-            dst_ref=kv_all.at[g, pl.ds((SPAN - d) * tok, tok), :],
-            send_sem=kv_ss.at[g, SPAN - d], recv_sem=kv_rs.at[g, SPAN - d],
-            device_id={"ctx": me + d}, device_id_type=MESH_ID,
-        )
-
-    def grad_copy(g, d):
-        return pltpu.make_async_remote_copy(
-            src_ref=gsend.at[g, SPAN - d], dst_ref=grecv.at[g, SPAN - d],
-            send_sem=g_ss.at[g, SPAN - d], recv_sem=g_rs.at[g, SPAN - d],
-            device_id={"ctx": me - d}, device_id_type=MESH_ID,
-        )
-
     def can_send(e):
         return me + e < n_ctx if e > 0 else me + e >= 0
 
@@ -128,10 +218,8 @@
     for k in range(1, n_dp):
         docs_copy(k).start()
     for g in range(HK):
-        for d in range(1, SPAN + 1):
-            @pl.when(me + d < n_ctx)
-            def _():
-                kv_copy(g, d).start()
+        for cond, copy in kv_sends(g):
+            pl.when(cond)(copy.start)
 
     doc_lo = jnp.sum(jnp.where(in_doc, starts, 0.0), axis=0, keepdims=True)
     kpos = (
@@ -157,12 +245,13 @@
     coef = LOSS_SCALE * 2.0 * prob / (floored * total[0:1, 0:1])
     weight = jnp.sum(picked[:, :tok] * coef, axis=0, keepdims=True)
     wcol_ref[...] = jnp.broadcast_to(as_column(weight), (tok, 128))
+    forward(0)
+    for c in big_in():
+        c.wait()
 
     def one_group(g, carry):
-        for d in range(1, SPAN + 1):
-            @pl.when(me >= d)
-            def _():
-                kv_copy(g, d).wait_recv()
+        for d in (1, 3):
+            kv_wait(g, d)
         kt_buf[...] = kv_all[g, :, 0:DH].T
         acc[...] = jnp.zeros_like(acc)
 
@@ -191,27 +280,40 @@
                 dq_ref[:, c] = dq[i * tok:(i + 1) * tok]
             acc[:, 0:DH] += jnp.dot(ds, q2, preferred_element_type=jnp.float32)
             acc[:, DH:2 * DH] += jnp.dot(p_low, og2, preferred_element_type=jnp.float32)
+
+            @pl.when((j == 0) & (g > 0))
+            def _():
+                combine(g - 1)
+
+            @pl.when((j == group // PAIR - 2) & (g < HK - 1))
+            def _():
+                forward(g + 1)
+
             return carry
 
         lax.fori_loop(0, group // PAIR, one_pair, 0)
-        acc[:, 0:DH] = acc[:, 0:DH] * scale
         for d in range(1, SPAN + 1):
             lo = (SPAN - d) * tok
-            @pl.when(me >= d)
+            gsend[g, SPAN - d, :, 0:DH] = (acc[lo:lo + tok, 0:DH] * scale).astype(jnp.bfloat16)
+            gsend[g, SPAN - d, :, DH:2 * DH] = acc[lo:lo + tok, DH:2 * DH].astype(jnp.bfloat16)
+        for cond, copy in exchange_copies(g):
+            pl.when(cond)(copy.start)
+        gown[g, :, 0:DH] = acc[SPAN * tok:, 0:DH] * scale
+        gown[g, :, DH:2 * DH] = acc[SPAN * tok:, DH:2 * DH]
+        return carry
+
+    lax.fori_loop(0, HK, one_group, 0)
+    combine(HK - 1)
+
+    for g in range(HK):
+        arrivals = ((0, even), (1, me - parity + 2 < n_ctx), (2, me - parity + 4 < n_ctx))
+        for slot, cond in arrivals:
+            @pl.when(cond)
             def _():
-                gsend[g, SPAN - d] = acc[lo:lo + tok, :].astype(jnp.bfloat16)
-                grad_copy(g, d).start()
-        gown[g] = acc[SPAN * tok:, :]
-        return carry
-
-    lax.fori_loop(0, HK, one_group, 0)
-
-    for g in range(HK):
-        for d in range(1, SPAN + 1):
-            @pl.when(me + d < n_ctx)
-            def _():
-                grad_copy(g, d).wait_recv()
-                gown[g] += grecv[g, SPAN - d].astype(jnp.float32)
+                remote(
+                    csend.at[g, 0], grecv.at[g, slot], g_ss.at[g, 0], g_rs.at[g, slot], partner
+                ).wait_recv()
+                gown[g] += grecv[g, slot].astype(jnp.float32)
         out = gown[g].astype(jnp.bfloat16)
         dkv_ref[:, g * DH:(g + 1) * DH] = out[:, 0:DH]
         dkv_ref[:, (HK + g) * DH:(HK + g + 1) * DH] = out[:, DH:2 * DH]
@@ -223,14 +325,9 @@
     for k in range(1, n_dp):
         docs_copy(k).wait_send()
     for g in range(HK):
-        for d in range(1, SPAN + 1):
-            @pl.when(me + d < n_ctx)
-            def _():
-                kv_copy(g, d).wait_send()
-
-            @pl.when(me >= d)
-            def _():
-                grad_copy(g, d).wait_send()
+        sent = kv_sends(g) + [f[1:] for f in kv_forwards(g)] + exchange_copies(g) + final_copies(g)
+        for cond, copy in sent:
+            pl.when(cond)(copy.wait_send)
 
 
 def local(n_ctx, n_dp, query, key_value, upstream, log_ratio, doc_starts, answer_counts):
@@ -247,9 +344,14 @@
             jax.ShapeDtypeStruct(query.shape[1:], bf16),
             jax.ShapeDtypeStruct(key_value.shape[1:], bf16),
         ),
-        in_specs=[vmem] * 6,
+        in_specs=[pl.BlockSpec(memory_space=pltpu.HBM)] * 6,
         out_specs=(vmem, vmem),
         scratch_shapes=[
+            pltpu.VMEM(query.shape[1:], bf16),
+            pltpu.VMEM(upstream.shape[1:], bf16),
+            pltpu.VMEM(log_ratio.shape, f32),
+            pltpu.VMEM(doc_starts.shape, jnp.int32),
+            pltpu.VMEM(answer_counts.shape, jnp.int32),
             pltpu.VMEM((HK, window, 2 * DH), bf16),
             pltpu.VMEM((DH, window), bf16),
             pltpu.VMEM((window, PAIR * tok), f32),
@@ -257,12 +359,15 @@
             pltpu.VMEM((window, 2 * DH), f32),
             pltpu.VMEM((HK, tok, 2 * DH), f32),
             pltpu.VMEM((HK, SPAN, tok, 2 * DH), bf16),
-            pltpu.VMEM((HK, SPAN, tok, 2 * DH), bf16),
+            pltpu.VMEM((HK, 2, tok, 2 * DH), bf16),
+            pltpu.VMEM((HK, 2, tok, 2 * DH), bf16),
+            pltpu.VMEM((HK, 3, tok, 2 * DH), bf16),
             pltpu.VMEM((slots, 128), f32),
             pltpu.VMEM((2 * SPAN + 1, slots, 128), f32),
             pltpu.VMEM((8, 128), f32),
             pltpu.VMEM((max(n_dp - 1, 1), 8, 128), f32),
-            sem((HK, SPAN)), sem((HK, SPAN)), sem((HK, SPAN)), sem((HK, SPAN)),
+            sem((5 + 2 * HK,)), sem((HK, 5)), sem((HK, SPAN)),
+            sem((HK, 2)), sem((HK, 2)), sem((HK, 3)), sem((HK, 3)),
             sem((2 * SPAN + 1,)), sem((2 * SPAN + 1,)),
             sem((max(n_dp - 1, 1),)), sem((max(n_dp - 1, 1),)),
         ],

time: 68.7 us -> 60.4 us (0.88)
  Pallas kernels: 59.7 us -> 51.6 us
    pallas_call x1, Pallas kernels: 59.7 us -> 51.6 us  [local(): pl.pallas_call(partial(kernel, n_ctx, n_dp), out_shape=(jax.ShapeDtypeStr...]
where the time goes in v2:
time: 60.4 us; the launch traced here: 60 us
  Pallas kernels  51.6 us (85%)
  local copies, waits for them, and re-layouts  7.68 us (13%)
  between operations  0.65 us (1%)
    pallas_call x1, Pallas kernels, local(): pl.pallas_call(partial(kernel, n_ctx, n_dp), out_shape=(jax.ShapeDtypeStr...  51.6 us
    unnamed x14, local copies, waits for them, and re-layouts  7.68 us

profile of v2, /device:TPU:2, one launch (start us, length us, event | category | flops | bytes accessed | tf_op | source)
XLA Modules:
  0.0 60.0 jit_solution(11475104078922766725)
XLA Ops:
  0.6 0.0 copy-start
  0.6 1.4 %copy-done = bf16[1,192,4096]{2,1,0:T(8,128)(2,1)S(1)} copy-done((bf16[1,192,4096]{2,1,0:T(8,128)(2,1)S(1)}, bf16[1,192,4096]{2,1,0:T(8,128)(2,1)}, u32[]{:S(2)}) %copy-start) | copy-done | bytes 1572888
  2.0 0.0 copy-start.1
  2.0 1.4 %copy-done.1 = bf16[1,192,4096]{2,1,0:T(8,128)(2,1)S(1)} copy-done((bf16[1,192,4096]{2,1,0:T(8,128)(2,1)S(1)}, bf16[1,192,4096]{2,1,0:T(8,128)(2,1)}, u32[]{:S(2)}) %copy-start.1) | copy-done | bytes 1572888
  3.4 0.0 copy-start.2
  3.5 1.0 %copy-done.2 = bf16[1,192,1024]{2,1,0:T(8,128)(2,1)S(1)} copy-done((bf16[1,192,1024]{2,1,0:T(8,128)(2,1)S(1)}, bf16[1,192,1024]{2,1,0:T(8,128)(2,1)}, u32[]{:S(2)}) %copy-start.2) | copy-done | bytes 393240
  4.4 0.0 copy-start.3
  4.4 0.7 %copy-done.3 = f32[1,192]{1,0:T(1,128)S(1)} copy-done((f32[1,192]{1,0:T(1,128)S(1)}, f32[1,192]{1,0:T(1,128)}, u32[]{:S(2)}) %copy-start.3) | copy-done | bytes 792
  5.1 0.0 copy-start.4
  5.1 0.7 %copy-done.4 = s32[1,16]{1,0:T(1,128)S(1)} copy-done((s32[1,16]{1,0:T(1,128)S(1)}, s32[1,16]{1,0:T(1,128)}, u32[]{:S(2)}) %copy-start.4) | copy-done | bytes 88
  5.8 0.0 copy-start.5
  5.8 0.7 %copy-done.5 = s32[1,16]{1,0:T(1,128)S(1)} copy-done((s32[1,16]{1,0:T(1,128)S(1)}, s32[1,16]{1,0:T(1,128)}, u32[]{:S(2)}) %copy-start.5) | copy-done | bytes 88
  6.4 51.6 %shard_map.77 = (bf16[192,4096]{1,0:T(8,128)(2,1)S(1)}, bf16[192,1024]{1,0:T(8,128)(2,1)S(1)}) custom-call(bf16[192,4096]{1,0:T(8,128)(2,1)S(1)} %bitcast.7, bf16[192,1024]{1,0:T(8,128)(2,1)S(1)} %bitcast.9, bf16[192,4096]{1,0:T(8,128)(2,1)S(1)} %bitcast.8, f32[1,192]{1,0:T(1,128)S(1)} %copy-done.3, s32[1,16]{1,0:T(1,128)S(1)} %copy-done.4, ...), custom_call_target="tpu_custom_call" | custom-call | flops 7549747200 | bytes 8388608 | tf_op jit(solution)/shard_map/pallas_call | solution.py:341
  58.1 1.1 %copy.10 = bf16[1,192,4096]{2,1,0:T(8,128)(2,1)} copy(bf16[1,192,4096]{2,1,0:T(8,128)(2,1)S(1)} %bitcast.5) | data formatting | bytes 3145728
  59.2 0.7 %copy.11 = bf16[1,192,1024]{2,1,0:T(8,128)(2,1)} copy(bf16[1,192,1024]{2,1,0:T(8,128)(2,1)S(1)} %bitcast.6) | data formatting | bytes 786432
Async XLA Ops:
  0.6 1.4 %copy-start = (bf16[1,192,4096]{2,1,0:T(8,128)(2,1)S(1)}, bf16[1,192,4096]{2,1,0:T(8,128)(2,1)}, u32[]{:S(2)}) copy-start(bf16[1,192,4096]{2,1,0:T(8,128)(2,1)} %param.6) | copy-start | bytes 4718596
  2.0 1.4 %copy-start.1 = (bf16[1,192,4096]{2,1,0:T(8,128)(2,1)S(1)}, bf16[1,192,4096]{2,1,0:T(8,128)(2,1)}, u32[]{:S(2)}) copy-start(bf16[1,192,4096]{2,1,0:T(8,128)(2,1)} %param.8) | copy-start | bytes 4718596
  3.4 1.0 %copy-start.2 = (bf16[1,192,1024]{2,1,0:T(8,128)(2,1)S(1)}, bf16[1,192,1024]{2,1,0:T(8,128)(2,1)}, u32[]{:S(2)}) copy-start(bf16[1,192,1024]{2,1,0:T(8,128)(2,1)} %param.7) | copy-start | bytes 1179652
  4.4 0.7 %copy-start.3 = (f32[1,192]{1,0:T(1,128)S(1)}, f32[1,192]{1,0:T(1,128)}, u32[]{:S(2)}) copy-start(f32[1,192]{1,0:T(1,128)} %lr_hbm.1) | copy-start | bytes 2308
  5.1 0.7 %copy-start.4 = (s32[1,16]{1,0:T(1,128)S(1)}, s32[1,16]{1,0:T(1,128)}, u32[]{:S(2)}) copy-start(s32[1,16]{1,0:T(1,128)} %st_hbm.1) | copy-start | bytes 196
  5.8 0.7 %copy-start.5 = (s32[1,16]{1,0:T(1,128)S(1)}, s32[1,16]{1,0:T(1,128)}, u32[]{:S(2)}) copy-start(s32[1,16]{1,0:T(1,128)} %ct_hbm.1) | copy-start | bytes 196

commit v3 on v2

--- a/solution.py
+++ b/solution.py
@@ -12,7 +12,7 @@
 DH = 128
 SPAN = 4
 LOSS_SCALE = 65536
-PAIR = 2
+PAIR = 4
 MESH_ID = pl.DeviceIdType.MESH
 LOG2E = 1.4426950408889634
 
@@ -31,11 +31,11 @@
 def kernel(
     n_ctx, n_dp,
     q_hbm, kv_hbm, up_hbm, lr_hbm, st_hbm, ct_hbm,
-    dq_ref, dkv_ref,
-    q_ref, up_ref, lr_ref, st_ref, ct_ref,
+    dq_hbm, dkv_hbm,
+    dq_ref, dkv_ref, q_ref, up_ref, lr_ref, st_ref, ct_ref,
     kv_all, kt_buf, bias, wcol_ref, acc, gown, gsend, xrecv, csend, grecv,
     psend, precv, dsend, drecv,
-    in_s, kv_ss, kv_rs, x_ss, x_rs, g_ss, g_rs, p_ss, p_rs, d_ss, d_rs,
+    in_s, out_s, kv_ss, kv_rs, x_ss, x_rs, g_ss, g_rs, p_ss, p_rs, d_ss, d_rs,
 ):
     tok = q_ref.shape[0]
     slots = st_ref.shape[1]
@@ -184,6 +184,10 @@
             add(1, 3)
             final_copies(g)[2][1].start()
 
+    def dq_out(g):
+        cols = pl.ds(pl.multiple_of(g * (group * DH), DH), group * DH)
+        return pltpu.make_async_copy(dq_ref.at[:, cols], dq_hbm.at[:, cols], out_s.at[g])
+
     for c in small_in():
         c.wait()
     starts = as_column(st_ref[...].astype(jnp.float32))
@@ -192,8 +196,8 @@
     ends = ends + jnp.where(slot_col == slots - 1, jnp.float32(seq_len), 0.0)
     counts_row = ct_ref[...].astype(jnp.float32)
     counts = as_column(counts_row)
-    lane = lax.broadcasted_iota(jnp.int32, (1, width), 1)
-    pos = (me * tok + jnp.where(lane >= tok, lane - tok, lane)).astype(jnp.float32)
+    lane = lax.rem(lax.broadcasted_iota(jnp.int32, (1, width), 1), tok)
+    pos = (me * tok + lane).astype(jnp.float32)
     in_doc = (pos >= starts) & (pos < ends)
     picked = (in_doc & (pos >= ends - counts)).astype(jnp.float32)
     part = jnp.sum(picked[:, :tok] * lr_ref[...], axis=1, keepdims=True)
@@ -292,6 +296,7 @@
             return carry
 
         lax.fori_loop(0, group // PAIR, one_pair, 0)
+        dq_out(g).start()
         for d in range(1, SPAN + 1):
             lo = (SPAN - d) * tok
             gsend[g, SPAN - d, :, 0:DH] = (acc[lo:lo + tok, 0:DH] * scale).astype(jnp.bfloat16)
@@ -318,6 +323,8 @@
         dkv_ref[:, g * DH:(g + 1) * DH] = out[:, 0:DH]
         dkv_ref[:, (HK + g) * DH:(HK + g + 1) * DH] = out[:, DH:2 * DH]
 
+    dkv_out = pltpu.make_async_copy(dkv_ref, dkv_hbm, out_s.at[HK])
+    dkv_out.start()
     for e in offsets:
         @pl.when(can_send(e))
         def _():
@@ -328,6 +335,8 @@
         sent = kv_sends(g) + [f[1:] for f in kv_forwards(g)] + exchange_copies(g) + final_copies(g)
         for cond, copy in sent:
             pl.when(cond)(copy.wait_send)
+        dq_out(g).wait()
+    dkv_out.wait()
 
 
 def local(n_ctx, n_dp, query, key_value, upstream, log_ratio, doc_starts, answer_counts):
@@ -336,7 +345,7 @@
     window = (SPAN + 1) * tok
     f32, bf16 = jnp.float32, jnp.bfloat16
     sem = pltpu.SemaphoreType.DMA
-    vmem = pl.BlockSpec(memory_space=pltpu.VMEM)
+    hbm = pl.BlockSpec(memory_space=pltpu.HBM)
     flops = 10 * HQ * tok * window * DH
     d_query, d_kv = pl.pallas_call(
         partial(kernel, n_ctx, n_dp),
@@ -344,9 +353,11 @@
             jax.ShapeDtypeStruct(query.shape[1:], bf16),
             jax.ShapeDtypeStruct(key_value.shape[1:], bf16),
         ),
-        in_specs=[pl.BlockSpec(memory_space=pltpu.HBM)] * 6,
-        out_specs=(vmem, vmem),
+        in_specs=[hbm] * 6,
+        out_specs=(hbm, hbm),
         scratch_shapes=[
+            pltpu.VMEM(query.shape[1:], bf16),
+            pltpu.VMEM(key_value.shape[1:], bf16),
             pltpu.VMEM(query.shape[1:], bf16),
             pltpu.VMEM(upstream.shape[1:], bf16),
             pltpu.VMEM(log_ratio.shape, f32),
@@ -366,13 +377,13 @@
             pltpu.VMEM((2 * SPAN + 1, slots, 128), f32),
             pltpu.VMEM((8, 128), f32),
             pltpu.VMEM((max(n_dp - 1, 1), 8, 128), f32),
-            sem((5 + 2 * HK,)), sem((HK, 5)), sem((HK, SPAN)),
+            sem((5 + 2 * HK,)), sem((HK + 1,)), sem((HK, 5)), sem((HK, SPAN)),
             sem((HK, 2)), sem((HK, 2)), sem((HK, 3)), sem((HK, 3)),
             sem((2 * SPAN + 1,)), sem((2 * SPAN + 1,)),
             sem((max(n_dp - 1, 1),)), sem((max(n_dp - 1, 1),)),
         ],
         compiler_params=pltpu.CompilerParams(
-            collective_id=0, has_side_effects=True, vmem_limit_bytes=48 * 1024 * 1024
+            collective_id=0, has_side_effects=True, vmem_limit_bytes=64 * 1024 * 1024
         ),
         cost_estimate=pl.CostEstimate(
             flops=flops, bytes_accessed=8 * 1024 * 1024, transcendentals=HQ * tok * window

time: 60.4 us -> 53.1 us (0.88)
  local copies, waits for them, and re-layouts: 7.68 us -> 3.5 us
  Pallas kernels: 51.6 us -> 48.5 us
    unnamed x14 -> x4, local copies, waits for them, and re-layouts: 7.68 us -> 3.5 us
    pallas_call x1, Pallas kernels: 51.6 us -> 48.5 us  [local(): pl.pallas_call(partial(kernel, n_ctx, n_dp), out_shape=(jax.ShapeDtypeStr...]
where the time goes in v3:
time: 53.1 us; the launch traced here: 52.7 us
  Pallas kernels  48.5 us (91%)
  local copies, waits for them, and re-layouts  3.5 us (7%)
  between operations  0.65 us (1%)
    pallas_call x1, Pallas kernels, local(): pl.pallas_call(partial(kernel, n_ctx, n_dp), out_shape=(jax.ShapeDtypeStr...  48.5 us
    unnamed x4, local copies, waits for them, and re-layouts  3.5 us

profile of v3, /device:TPU:2, one launch (start us, length us, event | category | flops | bytes accessed | tf_op | source)
XLA Modules:
  0.0 52.7 jit_solution(16162349654130213598)
XLA Ops:
  0.6 48.5 %shard_map.77 = (bf16[192,4096]{1,0:T(8,128)(2,1)}, bf16[192,1024]{1,0:T(8,128)(2,1)}) custom-call(bf16[192,4096]{1,0:T(8,128)(2,1)} %bitcast.7, bf16[192,1024]{1,0:T(8,128)(2,1)} %bitcast.9, bf16[192,4096]{1,0:T(8,128)(2,1)} %bitcast.8, f32[1,192]{1,0:T(1,128)} %lr_hbm.1, s32[1,16]{1,0:T(1,128)} %st_hbm.1, s32[1,16]{1,0:T(1,128)} %ct_hbm.1), custom_call_target="tpu_custom_call" | custom-call | flops 7549747200 | bytes 8388608 | tf_op jit(solution)/shard_map/pallas_call | solution.py:350
  49.2 0.0 copy-start
  49.2 2.8 %copy.10 = bf16[1,192,4096]{2,1,0:T(8,128)(2,1)} copy(bf16[1,192,4096]{2,1,0:T(8,128)(2,1)} %bitcast.5) | data formatting | bytes 3145728
  52.0 0.0 copy-done
  52.0 0.7 %copy.11 = bf16[1,192,1024]{2,1,0:T(8,128)(2,1)} copy(bf16[1,192,1024]{2,1,0:T(8,128)(2,1)S(1)} %bitcast.6) | data formatting | bytes 786432
Async XLA Ops:
  49.2 2.8 %copy-start = (bf16[192,1024]{1,0:T(8,128)(2,1)S(1)}, bf16[192,1024]{1,0:T(8,128)(2,1)}, u32[]{:S(2)}) copy-start(bf16[192,1024]{1,0:T(8,128)(2,1)} %get-tuple-element.5) | copy-start | bytes 1179652

commit v4 on v3

--- a/solution.py
+++ b/solution.py
@@ -196,7 +196,9 @@
     ends = ends + jnp.where(slot_col == slots - 1, jnp.float32(seq_len), 0.0)
     counts_row = ct_ref[...].astype(jnp.float32)
     counts = as_column(counts_row)
-    lane = lax.rem(lax.broadcasted_iota(jnp.int32, (1, width), 1), tok)
+    lane = lax.broadcasted_iota(jnp.int32, (1, width), 1)
+    for i in range(PAIR - 1, 0, -1):
+        lane = jnp.where(lane >= i * tok, lane - i * tok, lane)
     pos = (me * tok + lane).astype(jnp.float32)
     in_doc = (pos >= starts) & (pos < ends)
     picked = (in_doc & (pos >= ends - counts)).astype(jnp.float32)
@@ -221,15 +223,20 @@
             part_copy(e).start()
     for k in range(1, n_dp):
         docs_copy(k).start()
-    for g in range(HK):
+    def send_kv(g):
         for cond, copy in kv_sends(g):
             pl.when(cond)(copy.start)
 
+    send_kv(0)
+
     doc_lo = jnp.sum(jnp.where(in_doc, starts, 0.0), axis=0, keepdims=True)
-    kpos = (
-        (me - SPAN) * tok + lax.broadcasted_iota(jnp.int32, ((SPAN + 1) * tok, 1), 0)
-    ).astype(jnp.float32)
-    bias[...] = jnp.where((kpos >= doc_lo) & (kpos <= pos), 0.0, -1e30)
+    row = lax.broadcasted_iota(jnp.int32, (tok, 1), 0)
+    tri = row <= lane
+    near = (me * tok + row).astype(jnp.float32)
+    near = jnp.where(tri, near, near - SPAN * tok)
+    bias[0:tok] = jnp.where(near >= doc_lo, 0.0, -1e30)
+    rest = lax.broadcasted_iota(jnp.int32, ((SPAN - 1) * tok, 1), 0) + (me - SPAN + 1) * tok
+    bias[tok:] = jnp.where(rest.astype(jnp.float32) >= doc_lo, 0.0, -1e30)
 
     for e in offsets:
         @pl.when(can_send(-e))
@@ -249,6 +256,7 @@
     coef = LOSS_SCALE * 2.0 * prob / (floored * total[0:1, 0:1])
     weight = jnp.sum(picked[:, :tok] * coef, axis=0, keepdims=True)
     wcol_ref[...] = jnp.broadcast_to(as_column(weight), (tok, 128))
+    send_kv(1)
     forward(0)
     for c in big_in():
         c.wait()
@@ -256,6 +264,10 @@
     def one_group(g, carry):
         for d in (1, 3):
             kv_wait(g, d)
+        @pl.when(g < HK - 2)
+        def _():
+            send_kv(g + 2)
+
         kt_buf[...] = kv_all[g, :, 0:DH].T
         acc[...] = jnp.zeros_like(acc)
 
@@ -266,25 +278,35 @@
             vals = kv_all[g, :, DH:2 * DH]
             q2 = jnp.concatenate([q_ref[:, c] for c in cols], axis=0)
             wcol = wcol_ref[...]
+            tri = lax.broadcasted_iota(jnp.int32, (tok, 1), 0) <= lane
             og2 = jnp.concatenate(
                 [(wcol * up_ref[:, c].astype(jnp.float32)).astype(jnp.bfloat16) for c in cols],
                 axis=0,
             )
-            s = dot_nt(keys, q2) * (scale * LOG2E) + bias[...]
+            def merged(full):
+                near = jnp.where(tri, full[SPAN * tok:], full[:tok])
+                return jnp.concatenate([near, full[tok:SPAN * tok]], axis=0)
+
+            def spread(x):
+                far = jnp.where(tri, 0.0, x[:tok]).astype(jnp.bfloat16)
+                own = jnp.where(tri, x[:tok], 0.0).astype(jnp.bfloat16)
+                return jnp.concatenate([far, x[tok:].astype(jnp.bfloat16), own], axis=0)
+
+            s = merged(dot_nt(keys, q2)) * (scale * LOG2E) + bias[...]
             e = jnp.exp2(s - jnp.max(s, axis=0, keepdims=True))
             inv = 1.0 / jnp.sum(e, axis=0, keepdims=True)
             p = e * inv
-            dp = dot_nt(vals, og2)
+            dp = merged(dot_nt(vals, og2))
             delta = jnp.sum(p * dp, axis=0, keepdims=True)
-            p_low = p.astype(jnp.bfloat16)
-            ds = (p * (dp - delta)).astype(jnp.bfloat16)
+            p_low = spread(p)
+            ds = spread(p * (dp - delta))
+            acc[:, 0:DH] += jnp.dot(ds, q2, preferred_element_type=jnp.float32)
+            acc[:, DH:2 * DH] += jnp.dot(p_low, og2, preferred_element_type=jnp.float32)
+
             dqt = jnp.dot(kt_buf[...], ds, preferred_element_type=jnp.float32) * scale
             dq = dqt.T.astype(jnp.bfloat16)
             for i, c in enumerate(cols):
                 dq_ref[:, c] = dq[i * tok:(i + 1) * tok]
-            acc[:, 0:DH] += jnp.dot(ds, q2, preferred_element_type=jnp.float32)
-            acc[:, DH:2 * DH] += jnp.dot(p_low, og2, preferred_element_type=jnp.float32)
-
             @pl.when((j == 0) & (g > 0))
             def _():
                 combine(g - 1)
@@ -365,7 +387,7 @@
             pltpu.VMEM(answer_counts.shape, jnp.int32),
             pltpu.VMEM((HK, window, 2 * DH), bf16),
             pltpu.VMEM((DH, window), bf16),
-            pltpu.VMEM((window, PAIR * tok), f32),
+            pltpu.VMEM((window - tok, PAIR * tok), f32),
             pltpu.VMEM((tok, 128), f32),
             pltpu.VMEM((window, 2 * DH), f32),
             pltpu.VMEM((HK, tok, 2 * DH), f32),

time: 53.1 us -> 49.3 us (0.928)
  Pallas kernels: 48.5 us -> 44.8 us
    pallas_call x1, Pallas kernels: 48.5 us -> 44.8 us  [local(): pl.pallas_call(partial(kernel, n_ctx, n_dp), out_shape=(jax.ShapeDtypeStr...]
where the time goes in v4:
time: 49.3 us; the launch traced here: 48.9 us
  Pallas kernels  44.8 us (91%)
  local copies, waits for them, and re-layouts  3.5 us (7%)
  between operations  0.65 us (1%)
    pallas_call x1, Pallas kernels, local(): pl.pallas_call(partial(kernel, n_ctx, n_dp), out_shape=(jax.ShapeDtypeStr...  44.8 us
    unnamed x4, local copies, waits for them, and re-layouts  3.5 us

profile of v4, /device:TPU:2, one launch (start us, length us, event | category | flops | bytes accessed | tf_op | source)
XLA Modules:
  0.0 48.9 jit_solution(5150210023808113)
XLA Ops:
  0.6 44.8 %shard_map.77 = (bf16[192,4096]{1,0:T(8,128)(2,1)}, bf16[192,1024]{1,0:T(8,128)(2,1)}) custom-call(bf16[192,4096]{1,0:T(8,128)(2,1)} %bitcast.7, bf16[192,1024]{1,0:T(8,128)(2,1)} %bitcast.9, bf16[192,4096]{1,0:T(8,128)(2,1)} %bitcast.8, f32[1,192]{1,0:T(1,128)} %lr_hbm.1, s32[1,16]{1,0:T(1,128)} %st_hbm.1, s32[1,16]{1,0:T(1,128)} %ct_hbm.1), custom_call_target="tpu_custom_call" | custom-call | flops 7549747200 | bytes 8388608 | tf_op jit(solution)/shard_map/pallas_call | solution.py:372
  45.4 0.0 copy-start
  45.4 2.8 %copy.10 = bf16[1,192,4096]{2,1,0:T(8,128)(2,1)} copy(bf16[1,192,4096]{2,1,0:T(8,128)(2,1)} %bitcast.5) | data formatting | bytes 3145728
  48.2 0.0 copy-done
  48.2 0.7 %copy.11 = bf16[1,192,1024]{2,1,0:T(8,128)(2,1)} copy(bf16[1,192,1024]{2,1,0:T(8,128)(2,1)S(1)} %bitcast.6) | data formatting | bytes 786432
Async XLA Ops:
  45.4 2.8 %copy-start = (bf16[192,1024]{1,0:T(8,128)(2,1)S(1)}, bf16[192,1024]{1,0:T(8,128)(2,1)}, u32[]{:S(2)}) copy-start(bf16[192,1024]{1,0:T(8,128)(2,1)} %get-tuple-element.5) | copy-start | bytes 1179652
